TPU v7x, 32 devices: a whole 2x2x4 slice. The times are simulated.
32 devices in a mesh: grp: 2 (over x), prow: 16 (over z, y, core).
Axes of the slice: x: 2, y: 2, z: 4, core: 2. Of those that a mesh axis runs over, the one named last changes fastest.
Arguments:
- currents: bfloat16 [960, 128, 512], P(('grp', 'prow')), parts along dimension 0, may hold values from -6 to 6
- diag_inverse: bfloat16 [960, 128, 128], P(('grp', 'prow')), parts along dimension 0, as said below
- off_blocks: bfloat16 [960, 2, 128, 128], P(('grp', 'prow')), parts along dimension 0, may hold values from -0.25 to 0.25
- targets: int32 [960, 2], P(('grp', 'prow')), parts along dimension 0, may hold values from -1 to 479, as said below
Outputs:
- solution: bfloat16 [960, 128, 512], P(('grp', 'prow')), parts along dimension 0
There are 2 independent parts, one for each index of `grp`. A program takes and returns all parts, laid end to end along the dimension named above; each array names one. Nothing has to cross between parts.
Inputs may be any that keep to these rules, and one draw needn't show every extreme that they name: targets[n, 0] is -1 exactly for level-3 nodes, else a node of the next level held on the index of prow of n or one beside it; targets[n, 1] is -1 exactly for nodes of levels 2 and 3, else a node two levels up held on the index of prow of n or one beside it. diag_inverse is lower triangular with a positive diagonal.
All inputs are finite; a program needn't handle non-finite values.
Results may differ from a plain program's by a relative error of at most 0.0058.
Values may be sent and summed in bfloat16 or wider, within the bound.
A program may use at most 128 MiB of HBM per device.

v0:
```python
import functools

import jax
import jax.numpy as jnp
from jax import lax
from jax.experimental import pallas as pl
from jax.experimental.pallas import tpu as pltpu
from jax.sharding import PartitionSpec as P

MESH = pl.DeviceIdType.MESH
WIDTH = 128


def level_counts(per_device):
    top = per_device // 15
    return [8 * top, 4 * top, 2 * top, top], [0, 8 * top, 12 * top, 14 * top]


def kernel(
    cur, dia, off, tgt, out,
    curv, diav, offv, xs, acc1, acc2, acc3, sb1, sb2, sb3, rb1, rb2, rb3,
    prev1, prev2, prev3, last1, last2, last3,
    in_sem, out_sem, send_sem, recv_sem,
):
    peers = lax.axis_size("prow")
    me = lax.axis_index("prow")
    per_device = cur.shape[0]
    cnt, start = level_counts(per_device)
    chunks = curv.shape[0]
    accs, sbs, rbs = (acc1, acc2, acc3), (sb1, sb2, sb3), (rb1, rb2, rb3)
    prevs, lasts = (prev1, prev2, prev3), (last1, last2, last3)
    has = (me > 0, me < peers - 1)
    n0, n1, n2, n3 = cnt
    senders = start[3]

    def cur_copy(c, group):
        lo, n = ((0, n0), (n0, per_device - n0))[group]
        return pltpu.make_async_copy(
            cur.at[pl.ds(lo, n), :, pl.ds(pl.multiple_of(c * WIDTH, WIDTH), WIDTH)],
            curv.at[c, pl.ds(lo, n)],
            in_sem.at[group, c],
        )

    def weight_copies(group):
        lo, hi = ((0, n0), (n0, per_device))[group]
        hi_off = min(hi, senders)
        return (
            pltpu.make_async_copy(
                dia.at[pl.ds(lo, hi - lo)], diav.at[pl.ds(lo, hi - lo)], in_sem.at[group, chunks]
            ),
            pltpu.make_async_copy(
                off.at[pl.ds(lo, hi_off - lo)], offv.at[pl.ds(lo, hi_off - lo)],
                in_sem.at[group, chunks + 1],
            ),
        )

    def out_copy(level, c):
        lo, n = start[level], cnt[level]
        return pltpu.make_async_copy(
            xs.at[c, pl.ds(lo, n)],
            out.at[pl.ds(lo, n), :, pl.ds(pl.multiple_of(c * WIDTH, WIDTH), WIDTH)],
            out_sem.at[level, c],
        )

    def remote(p, c, d):
        neighbour = jnp.minimum(me + 1, peers - 1) if d else jnp.maximum(me - 1, 0)
        return pltpu.make_async_remote_copy(
            src_ref=sbs[p].at[c, d],
            dst_ref=rbs[p].at[c, 1 - d],
            send_sem=send_sem.at[p, c, d],
            recv_sem=recv_sem.at[p, c, 1 - d],
            device_id={"prow": neighbour},
            device_id_type=MESH,
        )

    for group in range(2):
        first, second = weight_copies(group)
        first.start()
        for c in range(chunks):
            cur_copy(c, group).start()
            if c == 0:
                second.start()

    barrier = pltpu.get_barrier_semaphore()
    for d in range(2):
        @pl.when(has[d])
        def _():
            pl.semaphore_signal(
                barrier, inc=1, device_id={"prow": me + (1 if d else -1)}, device_id_type=MESH
            )

    def column(p, i):
        if p == 0:
            return i, 0
        if p == 1:
            return i, jnp.where(i < n0, 1, 0)
        return n0 + i, jnp.where(i < n1, 1, 0)

    def aim(p, i):
        if isinstance(i, int):
            node, which = (i, 0) if p == 0 else (i, int(i < n0)) if p == 1 else (n0 + i, int(i < n1))
        else:
            node, which = column(p, i)
        return tgt[node, which]

    totals = (n0, n0 + n1, n1 + n2)

    def tables(p):
        total, slots = totals[p], cnt[p + 1]

        @pl.loop(0, total)
        def _(j):
            mine = aim(p, j)
            found = jnp.int32(total)
            for i in range(total):
                found = jnp.where((i < j) & (aim(p, i) == mine), i, found)
            prevs[p][j] = found

        @pl.loop(0, 3 * slots)
        def _(q):
            d = q // slots
            goal = (me + d - 1) * per_device + start[p + 1] + (q - d * slots)
            found = jnp.int32(total)
            for i in range(total):
                found = jnp.where(aim(p, i) == goal, i, found)
            lasts[p][q] = found

    def clear(p):
        @pl.loop(0, chunks)
        def _(c):
            accs[p][c, totals[p]] = jnp.zeros(accs[p].shape[2:], jnp.float32)

    def dot(a, b):
        return jnp.dot(a, b, preferred_element_type=jnp.float32)

    def solve(level, c):
        lo, n = start[level], cnt[level]
        step = min(n, 4)

        @pl.loop(0, n // step)
        def _(b):
            for u in range(step):
                s = b * step + u
                if level == 0:
                    reduced = curv[c, s]
                else:
                    p = level - 1
                    pending = accs[p][c, lasts[p][n + s]] + (
                        rbs[p][c, 0, s].astype(jnp.float32) + rbs[p][c, 1, s].astype(jnp.float32)
                    )
                    reduced = (curv[c, lo + s].astype(jnp.float32) - pending).astype(jnp.bfloat16)
                xs[c, lo + s] = dot(diav[lo + s], reduced).astype(jnp.bfloat16)

    def contribute(level, c):
        lo, n = start[level], cnt[level]
        step = min(n, 4)
        sn = diav.shape[1]

        def add(p, i, value):
            accs[p][c, i] = accs[p][c, prevs[p][i]] + value

        @pl.loop(0, n // step)
        def _(b):
            for u in range(step):
                j = b * step + u
                if level == 2:
                    add(2, n1 + j, dot(offv[lo + j, 0], xs[c, lo + j]))
                else:
                    both = dot(offv[lo + j].reshape(2 * sn, sn), xs[c, lo + j])
                    near, far = (j, j) if level == 0 else (n0 + j, j)
                    add(level, near, both[:sn])
                    add(level + 1, far, both[sn:])

    def send(p, c):
        slots = cnt[p + 1]
        for d in range(2):
            @pl.loop(0, slots)
            def _(s):
                sbs[p][c, d, s] = accs[p][c, lasts[p][2 * d * slots + s]].astype(jnp.bfloat16)

            @pl.when(has[d])
            def _():
                remote(p, c, d).start()

    def receive(p, c):
        for side in range(2):
            @pl.when(has[side])
            def _():
                remote(p, c, 1 - side).wait_recv()

            @pl.when(jnp.logical_not(has[side]))
            def _():
                rbs[p][c, side] = jnp.zeros(rbs[p].shape[2:], jnp.bfloat16)

    tables(0)
    for p in range(3):
        clear(p)
    tables(1)
    first, second = weight_copies(0)
    first.wait()
    second.wait()

    pl.semaphore_wait(barrier, jnp.where(has[0] & has[1], 2, 1))

    @pl.loop(0, chunks)
    def _(c):
        cur_copy(c, 0).wait()
        solve(0, c)
        out_copy(0, c).start()
        contribute(0, c)
        send(0, c)

    tables(2)
    first, second = weight_copies(1)
    first.wait()
    second.wait()

    @pl.loop(0, chunks)
    def _(c):
        cur_copy(c, 1).wait()

    for level in range(1, 4):
        @pl.loop(0, chunks)
        def _(c):
            receive(level - 1, c)
            solve(level, c)
            out_copy(level, c).start()
            if level < 3:
                contribute(level, c)
                send(level, c)

    @pl.loop(0, chunks)
    def _(c):
        for level in range(4):
            out_copy(level, c).wait()
        for p in range(3):
            for d in range(2):
                @pl.when(has[d])
                def _():
                    remote(p, c, d).wait_send()


def on_device(currents, diag_inverse, off_blocks, targets):
    per_device, sn, rhs = currents.shape
    cnt, start = level_counts(per_device)
    n0, n1, n2, n3 = cnt
    chunks = rhs // WIDTH
    totals = (n0, n0 + n1, n1 + n2)
    bf16, f32, i32 = jnp.bfloat16, jnp.float32, jnp.int32
    scratch = [
        pltpu.VMEM((chunks, per_device, sn, WIDTH), bf16),
        pltpu.VMEM((per_device, sn, sn), bf16),
        pltpu.VMEM((start[3], 2, sn, sn), bf16),
        pltpu.VMEM((chunks, per_device, sn, WIDTH), bf16),
    ]
    scratch += [pltpu.VMEM((chunks, t + 1, sn, WIDTH), f32) for t in totals]
    for _ in range(2):
        scratch += [pltpu.VMEM((chunks, 2, n, sn, WIDTH), bf16) for n in cnt[1:]]
    scratch += [pltpu.SMEM((t,), i32) for t in totals]
    scratch += [pltpu.SMEM((3 * n,), i32) for n in cnt[1:]]
    scratch += [
        pltpu.SemaphoreType.DMA((2, chunks + 2)),
        pltpu.SemaphoreType.DMA((4, chunks)),
        pltpu.SemaphoreType.DMA((3, chunks, 2)),
        pltpu.SemaphoreType.DMA((3, chunks, 2)),
    ]
    anywhere = pl.BlockSpec(memory_space=pl.ANY)
    return pl.pallas_call(
        kernel,
        out_shape=jax.ShapeDtypeStruct(currents.shape, currents.dtype),
        in_specs=[anywhere, anywhere, anywhere, pl.BlockSpec(memory_space=pltpu.SMEM)],
        out_specs=anywhere,
        scratch_shapes=scratch,
        compiler_params=pltpu.CompilerParams(
            collective_id=0, has_side_effects=True, vmem_limit_bytes=56 * 1024 * 1024
        ),
    )(currents, diag_inverse, off_blocks, targets)


def solution(mesh):
    placed = (
        P(("grp", "prow"), None, None),
        P(("grp", "prow"), None, None),
        P(("grp", "prow"), None, None, None),
        P(("grp", "prow"), None),
    )
    return jax.shard_map(
        on_device,
        mesh=mesh,
        in_specs=placed,
        out_specs=P(("grp", "prow"), None, None),
        check_vma=False,
    )
```

profile of v0, /device:TPU:1, one launch (start us, length us, event | category | flops | bytes accessed | tf_op | source)
XLA Modules:
  0.0 53.8 jit_solution(14657888538982582094)
XLA Ops:
  0.0 1.4 %copy.5.tgt = s32[30,2]{1,0:T(8,128)} copy(s32[30,2]{0,1:T(2,128)} %param.7) | data formatting | bytes 480 | tf_op args[3]
  1.4 48.0 %shard_map.46 = bf16[30,128,512]{2,1,0:T(8,128)(2,1)} custom-call(bf16[30,128,512]{2,1,0:T(8,128)(2,1)} %cur.1, bf16[30,128,128]{2,1,0:T(8,128)(2,1)} %dia.1, bf16[30,2,128,128]{3,2,1,0:T(8,128)(2,1)} %off.1, s32[30,2]{1,0:T(8,128)} %copy.5.tgt), custom_call_target="tpu_custom_call" | custom-call | tf_op jit(solution)/shard_map/pallas_call | solution.py:268
  49.4 4.4 %copy.7 = bf16[30,128,512]{2,1,0:T(8,128)(2,1)} copy(bf16[30,128,512]{2,1,0:T(8,128)(2,1)} %shard_map.46) | data formatting | bytes 7864320
where the time goes:
time: 54.1 us; the launch traced here: 53.8 us
  Pallas kernels  48 us (89%)
  local copies, waits for them, and re-layouts  5.81 us (11%)
    pallas_call x1, Pallas kernels, on_device(): pl.pallas_call(kernel, out_shape=jax.ShapeDtypeStruct(currents.shape, cur...  48 us
    unnamed x2, local copies, waits for them, and re-layouts  5.81 us

commit v1 on v0

--- a/solution.py
+++ b/solution.py
@@ -9,6 +9,7 @@
 
 MESH = pl.DeviceIdType.MESH
 WIDTH = 128
+PIECES = 3
 
 
 def level_counts(per_device):
@@ -17,10 +18,10 @@
 
 
 def kernel(
-    cur, dia, off, tgt, out,
-    curv, diav, offv, xs, acc1, acc2, acc3, sb1, sb2, sb3, rb1, rb2, rb3,
+    cur, dia, off, tgt, xs,
+    curv, diav, offv, acc1, acc2, acc3, sb1, sb2, sb3, rb1, rb2, rb3,
     prev1, prev2, prev3, last1, last2, last3,
-    in_sem, out_sem, send_sem, recv_sem,
+    in_sem, send_sem, recv_sem,
 ):
     peers = lax.axis_size("prow")
     me = lax.axis_index("prow")
@@ -54,14 +55,6 @@
             ),
         )
 
-    def out_copy(level, c):
-        lo, n = start[level], cnt[level]
-        return pltpu.make_async_copy(
-            xs.at[c, pl.ds(lo, n)],
-            out.at[pl.ds(lo, n), :, pl.ds(pl.multiple_of(c * WIDTH, WIDTH), WIDTH)],
-            out_sem.at[level, c],
-        )
-
     def remote(p, c, d):
         neighbour = jnp.minimum(me + 1, peers - 1) if d else jnp.maximum(me - 1, 0)
         return pltpu.make_async_remote_copy(
@@ -101,7 +94,7 @@
             node, which = (i, 0) if p == 0 else (i, int(i < n0)) if p == 1 else (n0 + i, int(i < n1))
         else:
             node, which = column(p, i)
-        return tgt[node, which]
+        return tgt[which, node]
 
     totals = (n0, n0 + n1, n1 + n2)
 
@@ -151,7 +144,7 @@
                     reduced = (curv[c, lo + s].astype(jnp.float32) - pending).astype(jnp.bfloat16)
                 xs[c, lo + s] = dot(diav[lo + s], reduced).astype(jnp.bfloat16)
 
-    def contribute(level, c):
+    def contribute(level, c, which=0):
         lo, n = start[level], cnt[level]
         step = min(n, 4)
         sn = diav.shape[1]
@@ -163,13 +156,14 @@
         def _(b):
             for u in range(step):
                 j = b * step + u
-                if level == 2:
+                if level == 0:
+                    add(which, j, dot(offv[j, which], xs[c, j]))
+                elif level == 2:
                     add(2, n1 + j, dot(offv[lo + j, 0], xs[c, lo + j]))
                 else:
                     both = dot(offv[lo + j].reshape(2 * sn, sn), xs[c, lo + j])
-                    near, far = (j, j) if level == 0 else (n0 + j, j)
-                    add(level, near, both[:sn])
-                    add(level + 1, far, both[sn:])
+                    add(1, n0 + j, both[:sn])
+                    add(2, j, both[sn:])
 
     def send(p, c):
         slots = cnt[p + 1]
@@ -193,9 +187,7 @@
                 rbs[p][c, side] = jnp.zeros(rbs[p].shape[2:], jnp.bfloat16)
 
     tables(0)
-    for p in range(3):
-        clear(p)
-    tables(1)
+    clear(0)
     first, second = weight_copies(0)
     first.wait()
     second.wait()
@@ -206,11 +198,18 @@
     def _(c):
         cur_copy(c, 0).wait()
         solve(0, c)
-        out_copy(0, c).start()
         contribute(0, c)
         send(0, c)
 
+    clear(1)
+    clear(2)
+    tables(1)
     tables(2)
+
+    @pl.loop(0, chunks)
+    def _(c):
+        contribute(0, c, 1)
+
     first, second = weight_copies(1)
     first.wait()
     second.wait()
@@ -224,20 +223,35 @@
         def _(c):
             receive(level - 1, c)
             solve(level, c)
-            out_copy(level, c).start()
             if level < 3:
                 contribute(level, c)
                 send(level, c)
 
     @pl.loop(0, chunks)
     def _(c):
-        for level in range(4):
-            out_copy(level, c).wait()
         for p in range(3):
             for d in range(2):
                 @pl.when(has[d])
                 def _():
                     remote(p, c, d).wait_send()
+
+
+def write_out(solved, out, sem):
+    chunks, nodes = solved.shape[0], solved.shape[1]
+    part = nodes // PIECES
+    copies = [
+        pltpu.make_async_copy(
+            solved.at[c, pl.ds(k * part, part)],
+            out.at[pl.ds(k * part, part), :, pl.ds(c * WIDTH, WIDTH)],
+            sem.at[c, k],
+        )
+        for c in range(chunks)
+        for k in range(PIECES)
+    ]
+    for copy in copies:
+        copy.start()
+    for copy in copies:
+        copy.wait()
 
 
 def on_device(currents, diag_inverse, off_blocks, targets):
@@ -251,7 +265,6 @@
         pltpu.VMEM((chunks, per_device, sn, WIDTH), bf16),
         pltpu.VMEM((per_device, sn, sn), bf16),
         pltpu.VMEM((start[3], 2, sn, sn), bf16),
-        pltpu.VMEM((chunks, per_device, sn, WIDTH), bf16),
     ]
     scratch += [pltpu.VMEM((chunks, t + 1, sn, WIDTH), f32) for t in totals]
     for _ in range(2):
@@ -260,21 +273,28 @@
     scratch += [pltpu.SMEM((3 * n,), i32) for n in cnt[1:]]
     scratch += [
         pltpu.SemaphoreType.DMA((2, chunks + 2)),
-        pltpu.SemaphoreType.DMA((4, chunks)),
         pltpu.SemaphoreType.DMA((3, chunks, 2)),
         pltpu.SemaphoreType.DMA((3, chunks, 2)),
     ]
     anywhere = pl.BlockSpec(memory_space=pl.ANY)
-    return pl.pallas_call(
+    solved = pl.pallas_call(
         kernel,
-        out_shape=jax.ShapeDtypeStruct(currents.shape, currents.dtype),
+        out_shape=pltpu.VMEM((chunks, per_device, sn, WIDTH), bf16),
         in_specs=[anywhere, anywhere, anywhere, pl.BlockSpec(memory_space=pltpu.SMEM)],
-        out_specs=anywhere,
+        out_specs=pl.BlockSpec(memory_space=pltpu.VMEM),
         scratch_shapes=scratch,
         compiler_params=pltpu.CompilerParams(
             collective_id=0, has_side_effects=True, vmem_limit_bytes=56 * 1024 * 1024
         ),
-    )(currents, diag_inverse, off_blocks, targets)
+    )(currents, diag_inverse, off_blocks, targets.T)
+    return pl.pallas_call(
+        write_out,
+        out_shape=jax.ShapeDtypeStruct(currents.shape, currents.dtype),
+        in_specs=[anywhere],
+        out_specs=anywhere,
+        scratch_shapes=[pltpu.SemaphoreType.DMA((chunks, PIECES))],
+        compiler_params=pltpu.CompilerParams(vmem_limit_bytes=2 * 1024 * 1024),
+    )(pltpu.with_memory_space_constraint(solved, pltpu.VMEM))
 
 
 def solution(mesh):

time: 54.1 us -> 49.1 us (0.908)
  local copies, waits for them, and re-layouts: 5.81 us -> 0 us
  Pallas kernels: 48 us -> 48.9 us
    unnamed x2 -> x0, local copies, waits for them, and re-layouts: 5.81 us -> none
    pallas_call x1 -> x2, Pallas kernels: 48 us -> 48.9 us  [the longest x1 46.9 us: on_device(): pl.pallas_call(kernel, out_shape=pltpu.VMEM((chunks, per_device, sn, WIDT...]
where the time goes in v1:
time: 49.1 us; the launch traced here: 48.9 us
  Pallas kernels  48.9 us (100%)
    pallas_call x1, Pallas kernels, on_device(): pl.pallas_call(kernel, out_shape=pltpu.VMEM((chunks, per_device, sn, WIDT...  46.9 us
    pallas_call x1, Pallas kernels, on_device(): pl.pallas_call(write_out, out_shape=jax.ShapeDtypeStruct(currents.shape,...  2.02 us

profile of v1, /device:TPU:1, one launch (start us, length us, event | category | flops | bytes accessed | tf_op | source)
XLA Modules:
  0.0 48.9 jit_solution(16066984399018251270)
XLA Ops:
  0.0 46.9 %shard_map.46.solved = bf16[4,30,128,128]{3,2,1,0:T(8,128)(2,1)S(1)} custom-call(bf16[30,128,512]{2,1,0:T(8,128)(2,1)} %cur.1, bf16[30,128,128]{2,1,0:T(8,128)(2,1)} %dia.1, bf16[30,2,128,128]{3,2,1,0:T(8,128)(2,1)} %off.1, s32[2,30]{1,0:T(2,128)} %bitcast.1), custom_call_target="tpu_custom_call" | custom-call | tf_op jit(solution)/shard_map/pallas_call | solution.py:280
  46.9 2.0 %shard_map.47 = bf16[30,128,512]{2,1,0:T(8,128)(2,1)} custom-call(bf16[4,30,128,128]{3,2,1,0:T(8,128)(2,1)S(1)} %shard_map.46.solved), custom_call_target="tpu_custom_call" | custom-call | tf_op jit(solution)/shard_map/pallas_call | solution.py:290

commit v2 on v1

--- a/solution.py
+++ b/solution.py
@@ -9,7 +9,7 @@
 
 MESH = pl.DeviceIdType.MESH
 WIDTH = 128
-PIECES = 3
+PIECES = 6
 
 
 def level_counts(per_device):
@@ -66,13 +66,15 @@
             device_id_type=MESH,
         )
 
-    for group in range(2):
+    def load(group):
         first, second = weight_copies(group)
         first.start()
         for c in range(chunks):
             cur_copy(c, group).start()
             if c == 0:
                 second.start()
+
+    load(0)
 
     barrier = pltpu.get_barrier_semaphore()
     for d in range(2):
@@ -109,9 +111,14 @@
                 found = jnp.where((i < j) & (aim(p, i) == mine), i, found)
             prevs[p][j] = found
 
-        @pl.loop(0, 3 * slots)
+        chain_ends(p, 0)
+        chain_ends(p, 2)
+
+    def chain_ends(p, d):
+        total, slots = totals[p], cnt[p + 1]
+
+        @pl.loop(d * slots, (d + 1) * slots)
         def _(q):
-            d = q // slots
             goal = (me + d - 1) * per_device + start[p + 1] + (q - d * slots)
             found = jnp.int32(total)
             for i in range(total):
@@ -122,6 +129,9 @@
         @pl.loop(0, chunks)
         def _(c):
             accs[p][c, totals[p]] = jnp.zeros(accs[p].shape[2:], jnp.float32)
+
+    def columns(c):
+        return pl.ds(pl.multiple_of(c * WIDTH, WIDTH), WIDTH)
 
     def dot(a, b):
         return jnp.dot(a, b, preferred_element_type=jnp.float32)
@@ -142,7 +152,7 @@
                         rbs[p][c, 0, s].astype(jnp.float32) + rbs[p][c, 1, s].astype(jnp.float32)
                     )
                     reduced = (curv[c, lo + s].astype(jnp.float32) - pending).astype(jnp.bfloat16)
-                xs[c, lo + s] = dot(diav[lo + s], reduced).astype(jnp.bfloat16)
+                xs[lo + s, :, columns(c)] = dot(diav[lo + s], reduced).astype(jnp.bfloat16)
 
     def contribute(level, c, which=0):
         lo, n = start[level], cnt[level]
@@ -157,24 +167,29 @@
             for u in range(step):
                 j = b * step + u
                 if level == 0:
-                    add(which, j, dot(offv[j, which], xs[c, j]))
+                    add(which, j, dot(offv[j, which], xs[j, :, columns(c)]))
                 elif level == 2:
-                    add(2, n1 + j, dot(offv[lo + j, 0], xs[c, lo + j]))
+                    add(2, n1 + j, dot(offv[lo + j, 0], xs[lo + j, :, columns(c)]))
                 else:
-                    both = dot(offv[lo + j].reshape(2 * sn, sn), xs[c, lo + j])
+                    both = dot(offv[lo + j].reshape(2 * sn, sn), xs[lo + j, :, columns(c)])
                     add(1, n0 + j, both[:sn])
                     add(2, j, both[sn:])
 
     def send(p, c):
         slots = cnt[p + 1]
-        for d in range(2):
+        for k in range(2):
+            right = lax.rem(me + k, 2)
+
             @pl.loop(0, slots)
             def _(s):
-                sbs[p][c, d, s] = accs[p][c, lasts[p][2 * d * slots + s]].astype(jnp.bfloat16)
-
-            @pl.when(has[d])
-            def _():
-                remote(p, c, d).start()
+                sbs[p][c, right, s] = accs[p][c, lasts[p][2 * right * slots + s]].astype(
+                    jnp.bfloat16
+                )
+
+            for d in range(2):
+                @pl.when(has[d] & (right == d))
+                def _():
+                    remote(p, c, d).start()
 
     def receive(p, c):
         for side in range(2):
@@ -187,6 +202,7 @@
                 rbs[p][c, side] = jnp.zeros(rbs[p].shape[2:], jnp.bfloat16)
 
     tables(0)
+    load(1)
     clear(0)
     first, second = weight_copies(0)
     first.wait()
@@ -205,6 +221,8 @@
     clear(2)
     tables(1)
     tables(2)
+    for p in range(3):
+        chain_ends(p, 1)
 
     @pl.loop(0, chunks)
     def _(c):
@@ -237,15 +255,11 @@
 
 
 def write_out(solved, out, sem):
-    chunks, nodes = solved.shape[0], solved.shape[1]
-    part = nodes // PIECES
+    part = solved.shape[0] // PIECES
     copies = [
         pltpu.make_async_copy(
-            solved.at[c, pl.ds(k * part, part)],
-            out.at[pl.ds(k * part, part), :, pl.ds(c * WIDTH, WIDTH)],
-            sem.at[c, k],
+            solved.at[pl.ds(k * part, part)], out.at[pl.ds(k * part, part)], sem.at[k]
         )
-        for c in range(chunks)
         for k in range(PIECES)
     ]
     for copy in copies:
@@ -279,7 +293,7 @@
     anywhere = pl.BlockSpec(memory_space=pl.ANY)
     solved = pl.pallas_call(
         kernel,
-        out_shape=pltpu.VMEM((chunks, per_device, sn, WIDTH), bf16),
+        out_shape=pltpu.VMEM(currents.shape, bf16),
         in_specs=[anywhere, anywhere, anywhere, pl.BlockSpec(memory_space=pltpu.SMEM)],
         out_specs=pl.BlockSpec(memory_space=pltpu.VMEM),
         scratch_shapes=scratch,
@@ -292,7 +306,7 @@
         out_shape=jax.ShapeDtypeStruct(currents.shape, currents.dtype),
         in_specs=[anywhere],
         out_specs=anywhere,
-        scratch_shapes=[pltpu.SemaphoreType.DMA((chunks, PIECES))],
+        scratch_shapes=[pltpu.SemaphoreType.DMA((PIECES,))],
         compiler_params=pltpu.CompilerParams(vmem_limit_bytes=2 * 1024 * 1024),
     )(pltpu.with_memory_space_constraint(solved, pltpu.VMEM))
 

time: 49.1 us -> 49 us (level)
  no operation moved by 1% of the time
where the time goes in v2:
time: 49 us; the launch traced here: 48.8 us
  Pallas kernels  48.8 us (100%)
    pallas_call x1, Pallas kernels, on_device(): pl.pallas_call(kernel, out_shape=pltpu.VMEM(currents.shape, bf16), in_spe...  46.8 us
    pallas_call x1, Pallas kernels, on_device(): pl.pallas_call(write_out, out_shape=jax.ShapeDtypeStruct(currents.shape,...  1.97 us

profile of v2, /device:TPU:1, one launch (start us, length us, event | category | flops | bytes accessed | tf_op | source)
XLA Modules:
  0.0 48.8 jit_solution(15912261522696895591)
XLA Ops:
  0.0 46.8 %shard_map.46.solved = bf16[30,128,512]{2,1,0:T(8,128)(2,1)S(1)} custom-call(bf16[30,128,512]{2,1,0:T(8,128)(2,1)} %cur.1, bf16[30,128,128]{2,1,0:T(8,128)(2,1)} %dia.1, bf16[30,2,128,128]{3,2,1,0:T(8,128)(2,1)} %off.1, s32[2,30]{1,0:T(2,128)} %bitcast.1), custom_call_target="tpu_custom_call" | custom-call | tf_op jit(solution)/shard_map/pallas_call | solution.py:294
  46.8 2.0 %shard_map.47 = bf16[30,128,512]{2,1,0:T(8,128)(2,1)} custom-call(bf16[30,128,512]{2,1,0:T(8,128)(2,1)S(1)} %shard_map.46.solved), custom_call_target="tpu_custom_call" | custom-call | tf_op jit(solution)/shard_map/pallas_call | solution.py:304

commit v3 on v2

--- a/solution.py
+++ b/solution.py
@@ -138,7 +138,7 @@
 
     def solve(level, c):
         lo, n = start[level], cnt[level]
-        step = min(n, 4)
+        step = min(n, 8)
 
         @pl.loop(0, n // step)
         def _(b):
@@ -156,7 +156,7 @@
 
     def contribute(level, c, which=0):
         lo, n = start[level], cnt[level]
-        step = min(n, 4)
+        step = min(n, 8)
         sn = diav.shape[1]
 
         def add(p, i, value):

time: 49 us -> 48.4 us (0.988)
  Pallas kernels: 48.8 us -> 48.2 us
    pallas_call x1, Pallas kernels: 46.8 us -> 46.3 us  [on_device(): pl.pallas_call(kernel, out_shape=pltpu.VMEM(currents.shape, bf16), in_spe...]
where the time goes in v3:
time: 48.4 us; the launch traced here: 48.2 us
  Pallas kernels  48.2 us (100%)
    pallas_call x1, Pallas kernels, on_device(): pl.pallas_call(kernel, out_shape=pltpu.VMEM(currents.shape, bf16), in_spe...  46.3 us
    pallas_call x1, Pallas kernels, on_device(): pl.pallas_call(write_out, out_shape=jax.ShapeDtypeStruct(currents.shape,...  1.97 us

profile of v3, /device:TPU:1, one launch (start us, length us, event | category | flops | bytes accessed | tf_op | source)
XLA Modules:
  0.0 48.2 jit_solution(13920121075646125673)
XLA Ops:
  0.0 46.3 %shard_map.46.solved = bf16[30,128,512]{2,1,0:T(8,128)(2,1)S(1)} custom-call(bf16[30,128,512]{2,1,0:T(8,128)(2,1)} %cur.1, bf16[30,128,128]{2,1,0:T(8,128)(2,1)} %dia.1, bf16[30,2,128,128]{3,2,1,0:T(8,128)(2,1)} %off.1, s32[2,30]{1,0:T(2,128)} %bitcast.1), custom_call_target="tpu_custom_call" | custom-call | tf_op jit(solution)/shard_map/pallas_call | solution.py:294
  46.3 2.0 %shard_map.47 = bf16[30,128,512]{2,1,0:T(8,128)(2,1)} custom-call(bf16[30,128,512]{2,1,0:T(8,128)(2,1)S(1)} %shard_map.46.solved), custom_call_target="tpu_custom_call" | custom-call | tf_op jit(solution)/shard_map/pallas_call | solution.py:304
